TPU v7x, 128 devices: a whole 4x4x4 slice. The times are simulated.
128 devices in a mesh: grid: 16 (over y, x), mesh: 8 (over z, core).
Axes of the slice: x: 4, y: 4, z: 4, core: 2. Of those that a mesh axis runs over, the one named last changes fastest.
Arguments:
- grid_latent: bfloat16 [65536, 512], P(('grid', 'mesh')), may hold values from -6 to 6
- mesh_latent: bfloat16 [40960, 512], P(('grid', 'mesh')), may hold values from -6 to 6
- edge_latent: bfloat16 [128, 8, 256, 512], P(('grid', 'mesh')), may hold values from -6 to 6
- edge_sender: int32 [128, 8, 256], P(('grid', 'mesh')), may hold values from 0 to 511
- edge_receiver: int32 [128, 8, 256], P(('grid', 'mesh')), may hold values from 0 to 319
- edge_count: int32 [128, 8], P(('grid', 'mesh')), may hold values from 1 to 256, as said below
- edge_in_weight: bfloat16 [1536, 512], replicated, may hold values from -0.15625 to 0.15625
- edge_bias: bfloat16 [512], replicated, may hold values from -3 to 3
- edge_out_weight: bfloat16 [512, 512], replicated, may hold values from -0.25 to 0.25
- edge_gain: bfloat16 [512], replicated, may hold values from 0.25 to 1.75
- node_in_weight: bfloat16 [1024, 512], replicated, may hold values from -0.1875 to 0.1875
- node_bias: bfloat16 [512], replicated, may hold values from -3 to 3
- node_out_weight: bfloat16 [512, 512], replicated, may hold values from -0.25 to 0.25
- node_gain: bfloat16 [512], replicated, may hold values from 0.25 to 1.75
- grid_in_weight: bfloat16 [512, 512], replicated, may hold values from -0.25 to 0.25
- grid_bias: bfloat16 [512], replicated, may hold values from -3 to 3
- grid_out_weight: bfloat16 [512, 512], replicated, may hold values from -0.25 to 0.25
- grid_gain: bfloat16 [512], replicated, may hold values from 0.25 to 1.75
- mesh_cotangent: bfloat16 [40960, 512], P(('grid', 'mesh')), may hold values from -6 to 6
- grid_cotangent: bfloat16 [65536, 512], P(('grid', 'mesh')), may hold values from -6 to 6
Outputs:
- mesh_updated: bfloat16 [40960, 512], P(('grid', 'mesh'))
- grid_updated: bfloat16 [65536, 512], P(('grid', 'mesh'))
- grad_grid: bfloat16 [65536, 512], P(('grid', 'mesh'))
- grad_mesh: bfloat16 [40960, 512], P(('grid', 'mesh'))
- grad_edge: bfloat16 [128, 8, 256, 512], P(('grid', 'mesh'))
Inputs may be any that keep to these rules, and one draw needn't show every extreme that they name: `edge_count`: in each row p, at least one of the 8 blocks is full, at a position drawn from the seed.
All inputs are finite; a program needn't handle non-finite values.
Results may differ from a plain program's by a relative error of at most 0.02.
Values may be sent and summed in bfloat16 or wider, within the bound.
A program may use at most 128 MiB of HBM per device.

v0:
```python
import functools

import jax
import jax.numpy as jnp
from jax import lax
from jax.experimental import pallas as pl
from jax.experimental.pallas import tpu as pltpu
from jax.sharding import PartitionSpec as P

F32 = jnp.float32
BF16 = jnp.bfloat16


def mm(a, b):
    return jnp.dot(a, b, preferred_element_type=F32)


def mm_t(a, b):
    return lax.dot_general(a, b, (((1,), (1,)), ((), ())), preferred_element_type=F32)


def silu_pair(u):
    gate = 0.5 + 0.5 * jnp.tanh(0.5 * u)
    value = u * gate
    return value, gate + value * (1.0 - gate)


def normed(v):
    centred = v - jnp.mean(v, axis=-1, keepdims=True)
    inv = lax.rsqrt(jnp.mean(centred * centred, axis=-1, keepdims=True) + 1e-05)
    return centred * inv, inv


def normed_back(dx, unit, inv):
    along = jnp.mean(dx * unit, axis=-1, keepdims=True)
    return inv * (dx - jnp.mean(dx, axis=-1, keepdims=True) - unit * along)


def kernel(
    sizes,
    grid_hbm,
    mesh_hbm,
    edge_hbm,
    sender,
    receiver,
    count,
    edge_in_hbm,
    edge_out_hbm,
    node_in_hbm,
    node_out_hbm,
    grid_in_hbm,
    grid_out_hbm,
    vectors,
    mesh_cot_hbm,
    grid_cot_hbm,
    mesh_up_hbm,
    grid_up_hbm,
    grad_grid_hbm,
    grad_mesh_hbm,
    grad_edge_hbm,
    grid_v,
    mesh_v,
    edge_v,
    edge_in,
    edge_out,
    node_in,
    node_out,
    grid_in,
    grid_out,
    mesh_cot,
    grid_cot,
    grid_proj,
    recv_row,
    send_col,
    recv_col,
    first_v,
    slope_v,
    unit_v,
    inv_v,
    wanted_v,
    dfirst_v,
    rows_a,
    rows_c,
    part_b,
    pair_b,
    land_b,
    part_d,
    pair_d,
    land_d,
    node_first,
    node_mesh_grad,
    grid_grad,
    mesh_up,
    grid_up,
    grad_grid,
    grad_mesh,
    load_sem,
    out_sem,
    a_send,
    a_recv,
    b_send,
    b_pair,
    b_land,
    c_send,
    c_recv,
    d_send,
    d_pair,
    d_land,
):
    blocks, cap, width, mesh_rows, grid_rows = sizes
    lanes = 128
    fast = lax.axis_size("mesh")
    total = lax.axis_size("grid") * fast
    me = lax.axis_index("grid") * fast + lax.axis_index("mesh")
    core = lax.rem(me, 2)

    def at(shift):
        p = lax.rem(me + (shift + total), total)
        return (lax.div(p, fast), lax.rem(p, fast))

    twin = at(1 - 2 * core)

    def remote(src, dst, send_sem, recv_sem, device):
        return pltpu.make_async_remote_copy(
            src_ref=src,
            dst_ref=dst,
            send_sem=send_sem,
            recv_sem=recv_sem,
            device_id=device,
            device_id_type=pl.DeviceIdType.MESH,
        )

    wide = pl.ds(0, width)
    mid = pl.ds(width, width)
    last = pl.ds(2 * width, width)
    pairs = [
        (mesh_hbm, mesh_v),
        (edge_in_hbm.at[last], edge_in.at[last]),
        (grid_hbm, grid_v),
        (edge_in_hbm.at[mid], edge_in.at[mid]),
        (edge_in_hbm.at[wide], edge_in.at[wide]),
        (edge_hbm.at[0], edge_v),
        (edge_out_hbm, edge_out),
        (node_in_hbm, node_in),
        (node_out_hbm, node_out),
        (mesh_cot_hbm, mesh_cot),
        (grid_in_hbm, grid_in),
        (grid_out_hbm, grid_out),
        (grid_cot_hbm, grid_cot),
    ]
    loads = [pltpu.make_async_copy(src, dst, load_sem.at[i]) for i, (src, dst) in enumerate(pairs)]
    for load in loads:
        load.start()

    barrier = pltpu.get_barrier_semaphore()
    partners = [at(2), at(-2), at(4), at(-4), twin]
    for partner in partners:
        pl.semaphore_signal(
            barrier, inc=1, device_id=partner, device_id_type=pl.DeviceIdType.MESH
        )

    def vector(i):
        return vectors[i : i + 1, :]

    edge_bias, edge_gain, node_bias, node_gain, grid_bias, grid_gain = range(6)

    def spread_copy(i, rows, send, recv):
        routes = [
            (4, 2, at(2)),
            (4, 6, at(-2)),
            (4, 3 + 2 * core, twin),
            (2, 0, at(2)),
            (2, 1 + 2 * core, twin),
            (6, 5 + 2 * core, twin),
            (6, 8, at(-2)),
            (8 - 8 * core, 7 - 6 * core, twin),
        ]
        src, dst, device = routes[i]
        return remote(rows.at[src], rows.at[dst], send.at[i], recv.at[dst], device)

    def spread_arrived(slot, rows, send, recv):
        remote(rows.at[slot], rows.at[slot], send.at[0], recv.at[slot], twin).wait_recv()

    def spread_own(*bufs):
        for i in (0, 1, 2):
            spread_copy(i, *bufs).start()

    def spread_near(*bufs):
        spread_arrived(2, *bufs)
        spread_copy(3, *bufs).start()
        spread_copy(4, *bufs).start()
        spread_arrived(6, *bufs)

        @pl.when(core == 0)
        def _():
            spread_copy(6, *bufs).start()

        spread_copy(5, *bufs).start()

    def spread_far(*bufs):
        spread_arrived(0, *bufs)

        @pl.when(core == 0)
        def _():
            spread_arrived(8, *bufs)

        spread_copy(7, *bufs).start()

    def spread_sent(*bufs):
        for i in (0, 1, 2, 3, 4, 5, 7):
            spread_copy(i, *bufs).wait_send()

        @pl.when(core == 0)
        def _():
            spread_copy(6, *bufs).wait_send()

    def pair_copy(k, part, pair, land, send, pair_sem, land_sem):
        slot = lax.div(k - 1 + 2 * core, 2)
        return remote(part.at[k], pair.at[slot], send.at[k], pair_sem.at[slot], twin)

    def pair_arrived(slot, part, pair, land, send, pair_sem, land_sem):
        remote(pair.at[slot], pair.at[slot], send.at[1], pair_sem.at[slot], twin).wait_recv()

    def land_copy(i, part, pair, land, send, pair_sem, land_sem):
        src, k, device = [
            (part.at[6], 6, at(2)),
            (part.at[2], 2, at(-2)),
            (part.at[0], 0, at(-4)),
            (pair.at[4], 4, at(4)),
        ][i]
        return remote(src, land.at[i], send.at[k], land_sem.at[i], device)

    def join(k, part, pair):
        part[k] = (part[k].astype(F32) + pair[k // 2].astype(F32)).astype(BF16)

    def sum_near(i, *bufs):
        k = (6, 2)[i]
        pair_arrived(k // 2, *bufs)
        join(k, *bufs[:2])
        land_copy(i, *bufs).start()

    def sum_far_first(*bufs):
        @pl.when(core == 0)
        def _():
            land_copy(2, *bufs).start()

    def sum_far_last(*bufs):
        @pl.when(core == 0)
        def _():
            pair_arrived(4, *bufs)
            land_copy(3, *bufs).start()

        @pl.when(core == 1)
        def _():
            pair_arrived(0, *bufs)
            join(0, *bufs[:2])
            land_copy(2, *bufs).start()

    def summed(*bufs):
        part, pair, land = bufs[:3]

        @pl.when(core == 1)
        def _():
            land[3] = jnp.zeros((mesh_rows, width), BF16)

        pair_arrived(2, *bufs)
        for i in (0, 1, 2):
            land_copy(i, *bufs).wait_recv()

        @pl.when(core == 0)
        def _():
            land_copy(3, *bufs).wait_recv()

        value = part[4].astype(F32) + pair[2].astype(F32)
        for i in range(4):
            value = value + land[i].astype(F32)
        return value.astype(BF16)

    def sum_sent(*bufs):
        for k in (1, 3, 5, 7):
            pair_copy(k, *bufs).wait_send()
        for i in (0, 1, 2):
            land_copy(i, *bufs).wait_send()

        @pl.when(core == 0)
        def _():
            land_copy(3, *bufs).wait_send()

    spread_a = (rows_a, a_send, a_recv)
    spread_c = (rows_c, c_send, c_recv)
    sum_b = (part_b, pair_b, land_b, b_send, b_pair, b_land)
    sum_d = (part_d, pair_d, land_d, d_send, d_pair, d_land)

    def pick(column, n):
        tiles = -(-n // lanes)
        ids = jnp.concatenate([column] * tiles, axis=1)[:, :n]
        return jnp.where(lax.broadcasted_iota(jnp.int32, (cap, n), 1) == ids, 1.0, 0.0).astype(BF16)

    def put(row, n, start=0):
        ids = lax.broadcasted_iota(jnp.int32, (n, cap), 0) + start
        return jnp.where(ids == row, 1.0, 0.0).astype(BF16)

    loads[0].wait()
    loads[1].wait()
    rows_a[4] = mm(mesh_v[...], edge_in[last, :]).astype(BF16)
    pl.semaphore_wait(barrier, len(partners))
    spread_own(*spread_a)

    slot_index = lax.broadcasted_iota(jnp.int32, (1, cap), 1)
    for k in range(blocks):
        recv_row[k : k + 1, :] = jnp.where(slot_index < count[0, k], receiver[0, k : k + 1, :], -1)
    for src, dst in ((sender[0], send_col), (recv_row[...], recv_col)):
        turned = jnp.transpose(src)
        for k in range(blocks):
            dst[k] = jnp.broadcast_to(turned[:, k : k + 1], (cap, lanes))

    for load in loads[2:6]:
        load.wait()
    grid_proj[...] = mm(grid_v[...], edge_in[mid, :]).astype(BF16)

    def first_step(k, _):
        first_v[k] = (
            mm(edge_v[k], edge_in[wide, :])
            + mm(pick(send_col[k], grid_rows), grid_proj[...])
            + vector(edge_bias)
        )
        return 0

    lax.fori_loop(0, blocks, first_step, 0)
    loads[6].wait()

    def lane_block(t):
        return lax.rem(4 + t + t * t, 8)

    def twin_block(t):
        return lax.rem(lane_block(t) + 9 - 2 * core, 8)

    def forward_block(k):
        u = first_v[k] + mm(pick(recv_col[k], mesh_rows), rows_a[k])
        hidden, slope = silu_pair(u)
        slope_v[k] = slope.astype(BF16)
        unit, inv = normed(mm(hidden.astype(BF16), edge_out[...]))
        unit_v[k] = unit.astype(BF16)
        inv_v[k] = jnp.broadcast_to(inv, (cap, lanes))
        message = (edge_v[k].astype(F32) + vector(edge_gain) * unit).astype(BF16)
        part_b[k] = mm(put(recv_row[pl.ds(k, 1), :], mesh_rows), message).astype(BF16)

    def backward_block(k):
        wanted = mm(pick(recv_col[k], mesh_rows), rows_c[k])
        wanted_v[k] = wanted.astype(BF16)
        dv = normed_back(wanted * vector(edge_gain), unit_v[k].astype(F32), inv_v[k][:, :1])
        dhidden = mm_t(dv.astype(BF16), edge_out[...])
        dfirst = (dhidden * slope_v[k].astype(F32)).astype(BF16)
        dfirst_v[k] = dfirst
        part_d[k] = mm(put(recv_row[pl.ds(k, 1), :], mesh_rows), dfirst).astype(BF16)

    def all_blocks(block_fn, spread, sums):
        def step(t, _):
            @pl.when(t == 1)
            def _():
                spread_near(*spread)

            @pl.when(t == 2)
            def _():
                sum_near(0, *sums)

            @pl.when(t == 3)
            def _():
                sum_near(1, *sums)
                spread_far(*spread)

            block_fn(lane_block(t))

            @pl.when(t == 3)
            def _():
                sum_far_first(*sums)

            k = twin_block(t)
            spread_arrived(k, *spread)
            block_fn(k)
            pair_copy(k, *sums).start()
            return 0

        lax.fori_loop(0, blocks // 2, step, 0)
        sum_far_last(*sums)

    all_blocks(forward_block, spread_a, sum_b)

    for load in loads[7:10]:
        load.wait()
    node_first[...] = mm(mesh_v[...], node_in[wide, :]) + vector(node_bias)
    aggregate = summed(*sum_b)
    hidden, slope = silu_pair(node_first[...] + mm(aggregate, node_in[mid, :]))
    unit, inv = normed(mm(hidden.astype(BF16), node_out[...]))
    cot = mesh_cot[...].astype(F32)
    dv = normed_back(cot * vector(node_gain), unit, inv)
    dfirst = (mm_t(dv.astype(BF16), node_out[...]) * slope).astype(BF16)
    rows_c[4] = mm_t(dfirst, node_in[mid, :]).astype(BF16)
    spread_own(*spread_c)
    node_mesh_grad[...] = cot + mm_t(dfirst, node_in[wide, :])
    mesh_up[...] = (mesh_v[...].astype(F32) + vector(node_gain) * unit).astype(BF16)
    mesh_up_out = pltpu.make_async_copy(mesh_up, mesh_up_hbm, out_sem.at[blocks])
    mesh_up_out.start()

    for load in loads[10:13]:
        load.wait()

    def grid_step(i, _):
        rows = pl.ds(pl.multiple_of(i * cap, cap), cap)
        own = grid_v[rows, :]
        hidden, slope = silu_pair(mm(own, grid_in[...]) + vector(grid_bias))
        unit, inv = normed(mm(hidden.astype(BF16), grid_out[...]))
        grid_up[rows, :] = (own.astype(F32) + vector(grid_gain) * unit).astype(BF16)
        cot = grid_cot[rows, :].astype(F32)
        dv = normed_back(cot * vector(grid_gain), unit, inv)
        dfirst = (mm_t(dv.astype(BF16), grid_out[...]) * slope).astype(BF16)
        grid_grad[rows, :] = cot + mm_t(dfirst, grid_in[...])
        return 0

    lax.fori_loop(0, grid_rows // cap, grid_step, 0)
    grid_up_out = pltpu.make_async_copy(grid_up, grid_up_hbm, out_sem.at[blocks + 1])
    grid_up_out.start()

    all_blocks(backward_block, spread_c, sum_d)

    def edge_out_copy(k):
        return pltpu.make_async_copy(wanted_v.at[k], grad_edge_hbm.at[0, k], out_sem.at[k])

    def edge_step(k, _):
        wanted_v[k] = (
            wanted_v[k].astype(F32) + mm_t(dfirst_v[k], edge_in[wide, :])
        ).astype(BF16)
        edge_out_copy(k).start()
        return 0

    lax.fori_loop(0, blocks, edge_step, 0)

    def grid_sum_step(i, _):
        start = pl.multiple_of(i * cap, cap)
        rows = pl.ds(start, cap)
        value = mm(put(sender[0, 0:1, :], cap, start), dfirst_v[0])
        for k in range(1, blocks):
            value = value + mm(put(sender[0, k : k + 1, :], cap, start), dfirst_v[k])
        grad_grid[rows, :] = (
            grid_grad[rows, :] + mm_t(value.astype(BF16), edge_in[mid, :])
        ).astype(BF16)
        return 0

    lax.fori_loop(0, grid_rows // cap, grid_sum_step, 0)
    grad_grid_out = pltpu.make_async_copy(grad_grid, grad_grid_hbm, out_sem.at[blocks + 2])
    grad_grid_out.start()

    grad_mesh[...] = (node_mesh_grad[...] + mm_t(summed(*sum_d), edge_in[last, :])).astype(BF16)
    grad_mesh_out = pltpu.make_async_copy(grad_mesh, grad_mesh_hbm, out_sem.at[blocks + 3])
    grad_mesh_out.start()

    spread_sent(*spread_a)
    sum_sent(*sum_b)
    spread_sent(*spread_c)
    sum_sent(*sum_d)
    for k in range(blocks):
        edge_out_copy(k).wait()
    for copy in (mesh_up_out, grid_up_out, grad_grid_out, grad_mesh_out):
        copy.wait()


def on_device(
    grid_latent,
    mesh_latent,
    edge_latent,
    edge_sender,
    edge_receiver,
    edge_count,
    edge_in_weight,
    edge_bias,
    edge_out_weight,
    edge_gain,
    node_in_weight,
    node_bias,
    node_out_weight,
    node_gain,
    grid_in_weight,
    grid_bias,
    grid_out_weight,
    grid_gain,
    mesh_cotangent,
    grid_cotangent,
):
    _, blocks, cap, width = edge_latent.shape
    mesh_rows, grid_rows = mesh_latent.shape[0], grid_latent.shape[0]
    vectors = jnp.stack(
        [edge_bias, edge_gain, node_bias, node_gain, grid_bias, grid_gain]
    ).astype(F32)
    anywhere = pl.BlockSpec(memory_space=pl.ANY)
    vmem = pl.BlockSpec(memory_space=pltpu.VMEM)
    smem = pl.BlockSpec(memory_space=pltpu.SMEM)
    half = blocks // 2 + 1

    def buf(*shape, dtype=BF16):
        return pltpu.VMEM(shape, dtype)

    dma = lambda n: pltpu.SemaphoreType.DMA((n,))
    slots = (blocks, cap, width)
    block = (mesh_rows, width)
    scratch = [
        buf(grid_rows, width),
        buf(mesh_rows, width),
        buf(*slots),
        buf(3 * width, width),
        buf(width, width),
        buf(2 * width, width),
        buf(width, width),
        buf(width, width),
        buf(width, width),
        buf(mesh_rows, width),
        buf(grid_rows, width),
        buf(grid_rows, width),
        buf(blocks, cap, dtype=jnp.int32),
        buf(blocks, cap, 128, dtype=jnp.int32),
        buf(blocks, cap, 128, dtype=jnp.int32),
        buf(*slots, dtype=F32),
        buf(*slots),
        buf(*slots),
        buf(blocks, cap, 128, dtype=F32),
        buf(*slots),
        buf(*slots),
        buf(blocks + 1, *block),
        buf(blocks + 1, *block),
        buf(blocks, *block),
        buf(half, *block),
        buf(4, *block),
        buf(blocks, *block),
        buf(half, *block),
        buf(4, *block),
        buf(*block, dtype=F32),
        buf(*block, dtype=F32),
        buf(grid_rows, width, dtype=F32),
        buf(*block),
        buf(grid_rows, width),
        buf(grid_rows, width),
        buf(*block),
        dma(13),
        dma(blocks + 4),
        dma(8),
        dma(blocks + 1),
        dma(8),
        dma(half),
        dma(4),
        dma(8),
        dma(blocks + 1),
        dma(8),
        dma(half),
        dma(4),
    ]
    outs = [
        jax.ShapeDtypeStruct(mesh_latent.shape, BF16),
        jax.ShapeDtypeStruct(grid_latent.shape, BF16),
        jax.ShapeDtypeStruct(grid_latent.shape, BF16),
        jax.ShapeDtypeStruct(mesh_latent.shape, BF16),
        jax.ShapeDtypeStruct(edge_latent.shape, BF16),
    ]
    return pl.pallas_call(
        functools.partial(kernel, (blocks, cap, width, mesh_rows, grid_rows)),
        out_shape=outs,
        in_specs=[anywhere] * 3 + [vmem, vmem, smem] + [anywhere] * 6 + [vmem] + [anywhere] * 2,
        out_specs=[anywhere] * 5,
        scratch_shapes=scratch,
        compiler_params=pltpu.CompilerParams(
            collective_id=0, has_side_effects=True, vmem_limit_bytes=58 * 2**20
        ),
        cost_estimate=pl.CostEstimate(
            flops=13_000_000_000, bytes_accessed=16_000_000, transcendentals=3_000_000
        ),
        name="encoder",
    )(
        grid_latent,
        mesh_latent,
        edge_latent,
        edge_sender,
        edge_receiver,
        edge_count,
        edge_in_weight,
        edge_out_weight,
        node_in_weight,
        node_out_weight,
        grid_in_weight,
        grid_out_weight,
        vectors,
        mesh_cotangent,
        grid_cotangent,
    )


def solution(mesh):
    rows = P(("grid", "mesh"), None)
    wide = P(("grid", "mesh"), None, None)
    slots = P(("grid", "mesh"), None, None, None)
    return jax.shard_map(
        on_device,
        mesh=mesh,
        in_specs=(rows, rows, slots, wide, wide, rows) + (P(),) * 12 + (rows, rows),
        out_specs=(rows, rows, rows, rows, slots),
        check_vma=False,
    )
```

profile of v0, /device:TPU:1, one launch (start us, length us, event | category | flops | bytes accessed | tf_op | source)
XLA Modules:
  0.0 101.1 jit_solution(15912061942465703102)
XLA Ops:
  0.6 0.7 stack.21
  1.3 0.7 stack.22
  2.0 0.7 stack.23
  2.7 0.7 stack.24
  3.4 0.7 stack.25
  4.0 0.7 stack.26
  4.8 0.6 convert_element_type.3.vectors
  5.4 88.0 %encoder.1 = (bf16[320,512]{1,0:T(8,128)(2,1)}, bf16[512,512]{1,0:T(8,128)(2,1)}, bf16[512,512]{1,0:T(8,128)(2,1)}, bf16[320,512]{1,0:T(8,128)(2,1)}, bf16[1,8,256,512]{3,2,1,0:T(8,128)(2,1)}) custom-call(bf16[512,512]{1,0:T(8,128)(2,1)} %grid_hbm.1, bf16[320,512]{1,0:T(8,128)(2,1)} %mesh_hbm.1, bf16[1,8,256,512]{3,2,1,0:T(8,128)(2,1)} %edge_hbm.1, ...), custom_call_target="tpu_custom_call" | custom-call | flops 12999999488 | bytes 16000000 | tf_op jit(solution)/shard_map/encoder/pallas_call | solution.py:562
  93.4 0.0 copy-start.1
  93.4 0.0 copy-start
  93.4 1.9 %copy.30 = bf16[320,512]{1,0:T(8,128)(2,1)} copy(bf16[320,512]{1,0:T(8,128)(2,1)} %get-tuple-element.10) | data formatting | bytes 655360
  95.3 1.9 %copy.31 = bf16[512,512]{1,0:T(8,128)(2,1)} copy(bf16[512,512]{1,0:T(8,128)(2,1)} %get-tuple-element.11) | data formatting | bytes 1048576
  97.2 1.9 %copy.32 = bf16[512,512]{1,0:T(8,128)(2,1)} copy(bf16[512,512]{1,0:T(8,128)(2,1)} %get-tuple-element.12) | data formatting | bytes 1048576
  99.0 0.0 copy-done.1
  99.0 0.7 copy.33
  99.7 0.0 copy-done
  99.8 1.3 %copy.34 = bf16[1,8,256,512]{3,2,1,0:T(8,128)(2,1)} copy(bf16[1,8,256,512]{3,2,1,0:T(8,128)(2,1)S(1)} %copy-done) | data formatting | bytes 4194304
  (1 shorter events, 0.0 us)
Async XLA Ops:
  93.4 5.6 %copy-start.1 = (bf16[320,512]{1,0:T(8,128)(2,1)S(1)}, bf16[320,512]{1,0:T(8,128)(2,1)}, u32[]{:S(2)}) copy-start(bf16[320,512]{1,0:T(8,128)(2,1)} %get-tuple-element.13) | copy-start | bytes 983044
  93.4 6.3 %copy-start = (bf16[1,8,256,512]{3,2,1,0:T(8,128)(2,1)S(1)}, bf16[1,8,256,512]{3,2,1,0:T(8,128)(2,1)}, u32[]{:S(2)}) copy-start(bf16[1,8,256,512]{3,2,1,0:T(8,128)(2,1)} %get-tuple-element.14) | copy-start | bytes 6291460
where the time goes:
time: 101 us
  Pallas kernels  88 us (87%)
  local copies, waits for them, and re-layouts  11.8 us (12%)
    pallas_call x1, Pallas kernels, on_device(): pl.pallas_call(functools.partial(kernel, (blocks, cap, width, mesh_rows,...  88 us
    unnamed x9, local copies, waits for them, and re-layouts  7.65 us
    another operation x7, local copies, waits for them, and re-layouts, on_device(): jnp.stack([edge_bias, edge_gain, node_bias, node_gain, grid_bias, grid_ga...  4.12 us

commit v1 on v0

v1 whole, which is shorter than its diff:
```python
import functools
from types import SimpleNamespace

import jax
import jax.numpy as jnp
from jax import lax
from jax.experimental import pallas as pl
from jax.experimental.pallas import tpu as pltpu
from jax.sharding import PartitionSpec as P

F32 = jnp.float32
BF16 = jnp.bfloat16
PARTS = 2


def mm(a, b):
    return jnp.dot(a, b, preferred_element_type=F32)


def mm_t(a, b):
    return lax.dot_general(a, b, (((1,), (1,)), ((), ())), preferred_element_type=F32)


def silu_pair(u):
    gate = 0.5 + 0.5 * jnp.tanh(0.5 * u)
    value = u * gate
    return value, gate + value * (1.0 - gate)


def normed(v):
    centred = v - jnp.mean(v, axis=-1, keepdims=True)
    inv = lax.rsqrt(jnp.mean(centred * centred, axis=-1, keepdims=True) + 1e-05)
    return centred * inv, inv


def normed_back(dx, unit, inv):
    along = jnp.mean(dx * unit, axis=-1, keepdims=True)
    return inv * (dx - jnp.mean(dx, axis=-1, keepdims=True) - unit * along)


def kernel(
    sizes,
    grid_hbm,
    mesh_hbm,
    edge_hbm,
    sender,
    receiver,
    count,
    edge_in_hbm,
    edge_out_hbm,
    node_in_hbm,
    node_out_hbm,
    grid_in_hbm,
    grid_out_hbm,
    edge_bias,
    edge_gain,
    node_bias,
    node_gain,
    grid_bias,
    grid_gain,
    mesh_cot_hbm,
    grid_cot_hbm,
    mesh_up_hbm,
    grid_up_hbm,
    grad_grid_hbm,
    grad_mesh_hbm,
    grad_edge_hbm,
    grid_v,
    mesh_v,
    edge_v,
    edge_in,
    edge_out,
    node_in,
    node_out,
    grid_in,
    grid_out,
    mesh_cot,
    grid_cot,
    grid_proj,
    recv_row,
    send_col,
    recv_col,
    first_v,
    slope_v,
    unit_v,
    inv_v,
    wanted_v,
    dfirst_v,
    rows_a,
    rows_c,
    node_first,
    node_mesh_grad,
    grid_grad,
    mesh_up,
    grid_up,
    grad_grid,
    grad_mesh,
    load_sem,
    out_sem,
    a_send,
    a_recv,
    c_send,
    c_recv,
    *sum_refs,
):
    blocks, cap, width, mesh_rows, grid_rows = sizes
    lanes = 128
    fast = lax.axis_size("mesh")
    total = lax.axis_size("grid") * fast
    me = lax.axis_index("grid") * fast + lax.axis_index("mesh")
    core = lax.rem(me, 2)

    def at(shift):
        p = lax.rem(me + (shift + total), total)
        return (lax.div(p, fast), lax.rem(p, fast))

    twin = at(1 - 2 * core)

    def remote(src, dst, send_sem, recv_sem, device):
        return pltpu.make_async_remote_copy(
            src_ref=src,
            dst_ref=dst,
            send_sem=send_sem,
            recv_sem=recv_sem,
            device_id=device,
            device_id_type=pl.DeviceIdType.MESH,
        )

    wide = pl.ds(0, width)
    mid = pl.ds(width, width)
    last = pl.ds(2 * width, width)
    pairs = [
        (mesh_hbm, mesh_v),
        (edge_in_hbm.at[last], edge_in.at[last]),
        (grid_hbm, grid_v),
        (edge_in_hbm.at[mid], edge_in.at[mid]),
        (edge_in_hbm.at[wide], edge_in.at[wide]),
        (edge_hbm.at[0], edge_v),
        (edge_out_hbm, edge_out),
        (node_in_hbm, node_in),
        (node_out_hbm, node_out),
        (mesh_cot_hbm, mesh_cot),
        (grid_in_hbm, grid_in),
        (grid_out_hbm, grid_out),
        (grid_cot_hbm, grid_cot),
    ]
    loads = [pltpu.make_async_copy(src, dst, load_sem.at[i]) for i, (src, dst) in enumerate(pairs)]
    for load in loads[:2]:
        load.start()

    barrier = pltpu.get_barrier_semaphore()
    partners = [at(2), at(-2), at(4), at(-4), at(8), at(-8), twin]
    for partner in partners:
        pl.semaphore_signal(
            barrier, inc=1, device_id=partner, device_id_type=pl.DeviceIdType.MESH
        )

    def vector(ref):
        return ref[...].astype(F32).reshape(1, width)

    def spread_copy(i, part, spread):
        src, dst, device = [
            (4, 2, at(2)),
            (4, 6, at(-2)),
            (4, 3 + 2 * core, twin),
            (2, 0, at(2)),
            (2, 1 + 2 * core, twin),
            (6, 5 + 2 * core, twin),
            (6, 8, at(-2)),
            (8 - 8 * core, 7 - 6 * core, twin),
            (8, 0, at(8)),
        ][i]
        own = part_rows(part)
        return remote(
            spread.rows.at[src, own],
            spread.rows.at[dst, own],
            spread.send.at[i, part],
            spread.recv.at[dst, part],
            device,
        )

    def spread_arrived(slot, part, spread):
        own = spread.rows.at[slot, part_rows(part)]
        remote(own, own, spread.send.at[0, part], spread.recv.at[slot, part], twin).wait_recv()

    def spread_whole(slot, spread):
        for part in range(PARTS):
            spread_arrived(slot, part, spread)

    def spread_own(part, spread):
        for i in (0, 1, 2):
            spread_copy(i, part, spread).start()

    def spread_near(part, spread):
        spread_arrived(2, part, spread)
        spread_arrived(6, part, spread)

        @pl.when(core == 0)
        def _():
            spread_copy(6, part, spread).start()

        @pl.when(core == 1)
        def _():
            spread_copy(3, part, spread).start()

        spread_copy(4, part, spread).start()
        spread_copy(5, part, spread).start()

    def spread_far(part, spread):
        @pl.when(core == 0)
        def _():
            spread_arrived(8, part, spread)
            spread_copy(8, part, spread).start()

        @pl.when(core == 1)
        def _():
            spread_arrived(0, part, spread)

        spread_copy(7, part, spread).start()

    def spread_sent(spread):
        for part in range(PARTS):
            for i in (0, 1, 2, 4, 5, 7):
                spread_copy(i, part, spread).wait_send()

            @pl.when(core == 0)
            def _():
                spread_copy(6, part, spread).wait_send()
                spread_copy(8, part, spread).wait_send()

            @pl.when(core == 1)
            def _():
                spread_copy(3, part, spread).wait_send()

    def pair_copy(k, sums):
        slot = lax.div(k - 1 + 2 * core, 2)
        return remote(
            sums.part.at[k], sums.pair.at[slot], sums.send.at[k], sums.pair_recv.at[slot], twin
        )

    def pair_arrived(slot, sums):
        own = sums.pair.at[slot]
        remote(own, own, sums.send.at[1], sums.pair_recv.at[slot], twin).wait_recv()

    def near_copy(i, sums):
        k, device = [(6, at(2)), (2, at(-2))][i]
        return remote(
            sums.part.at[k], sums.land.at[i], sums.send.at[k], sums.near_recv.at[i], device
        )

    def cross_copy(part, sums):
        own = part_rows(part)
        return remote(
            sums.pair.at[4, own],
            sums.cross.at[own],
            sums.cross_send.at[part],
            sums.cross_recv.at[part],
            at(8),
        )

    def far_copy(part, sums):
        own = part_rows(part)
        return remote(
            sums.part.at[0, own],
            sums.land.at[2, own],
            sums.far_send.at[part],
            sums.far_recv.at[part],
            at(-4),
        )

    def sum_near(i, sums):
        k = (6, 2)[i]
        pair_arrived(k // 2, sums)
        sums.part[k] = (sums.part[k].astype(F32) + sums.pair[k // 2].astype(F32)).astype(BF16)
        near_copy(i, sums).start()

    def sum_cross(sums):
        @pl.when(core == 0)
        def _():
            pair_arrived(4, sums)
            for part in range(PARTS):
                cross_copy(part, sums).start()

    def sum_far(sums):
        def join_part(part, more):
            own = part_rows(part)
            sums.part[0, own] = (sums.part[0, own].astype(F32) + more.astype(F32)).astype(BF16)
            far_copy(part, sums).start()

        @pl.when(core == 0)
        def _():
            for part in range(PARTS):
                cross_copy(part, sums).wait_recv()
                join_part(part, sums.cross[part_rows(part)])

        @pl.when(core == 1)
        def _():
            pair_arrived(0, sums)
            for part in range(PARTS):
                join_part(part, sums.pair[0, part_rows(part)])

    def sum_near_wait(sums):
        pair_arrived(2, sums)
        for i in (0, 1):
            near_copy(i, sums).wait_recv()

    def summed(part, sums):
        far_copy(part, sums).wait_recv()
        own = part_rows(part)
        value = sums.part[4, own].astype(F32) + sums.pair[2, own].astype(F32)
        for i in range(3):
            value = value + sums.land[i, own].astype(F32)
        return value.astype(BF16)

    def sum_sent(sums):
        for k in (1, 3, 5, 7):
            pair_copy(k, sums).wait_send()
        for i in (0, 1):
            near_copy(i, sums).wait_send()
        for part in range(PARTS):
            far_copy(part, sums).wait_send()

        @pl.when(core == 0)
        def _():
            for part in range(PARTS):
                cross_copy(part, sums).wait_send()

    def part_rows(part):
        rows = mesh_rows // PARTS
        return pl.ds(pl.multiple_of(part * rows, rows), rows)

    spread_a = SimpleNamespace(rows=rows_a, send=a_send, recv=a_recv)
    spread_c = SimpleNamespace(rows=rows_c, send=c_send, recv=c_recv)
    sum_b, sum_d = [
        SimpleNamespace(
            part=refs[0],
            pair=refs[1],
            land=refs[2],
            cross=refs[3],
            send=refs[4],
            pair_recv=refs[5],
            near_recv=refs[6],
            far_send=refs[7],
            far_recv=refs[8],
            cross_send=refs[9],
            cross_recv=refs[10],
        )
        for refs in (sum_refs[:11], sum_refs[11:])
    ]

    def pick(column, n):
        tiles = -(-n // lanes)
        ids = jnp.concatenate([column] * tiles, axis=1)[:, :n]
        return jnp.where(lax.broadcasted_iota(jnp.int32, (cap, n), 1) == ids, 1.0, 0.0).astype(BF16)

    def put(row, n, start=0):
        ids = lax.broadcasted_iota(jnp.int32, (n, cap), 0) + start
        return jnp.where(ids == row, 1.0, 0.0).astype(BF16)

    loads[0].wait()
    loads[1].wait()
    for load in loads[2:]:
        load.start()
    rows_a[4] = mm(mesh_v[...], edge_in[last, :]).astype(BF16)
    pl.semaphore_wait(barrier, len(partners))
    for part in range(PARTS):
        spread_own(part, spread_a)

    slot_index = lax.broadcasted_iota(jnp.int32, (1, cap), 1)
    for k in range(blocks):
        recv_row[k : k + 1, :] = jnp.where(slot_index < count[0, k], receiver[0, k : k + 1, :], -1)
    for src, dst in ((sender[0], send_col), (recv_row[...], recv_col)):
        turned = jnp.transpose(src)
        for k in range(blocks):
            dst[k] = jnp.broadcast_to(turned[:, k : k + 1], (cap, lanes))

    for load in loads[2:6]:
        load.wait()
    grid_proj[...] = mm(grid_v[...], edge_in[mid, :]).astype(BF16)

    def first_step(k, _):
        first_v[k] = (
            mm(edge_v[k], edge_in[wide, :])
            + mm(pick(send_col[k], grid_rows), grid_proj[...])
            + vector(edge_bias)
        )
        return 0

    lax.fori_loop(0, blocks, first_step, 0)
    loads[6].wait()

    def step_blocks(t):
        lane = lax.rem(4 + t + t * t, 8)
        other = lax.rem(lane + 9 - 2 * core, 8)
        swap = lax.div(t, 3) * (other - lane)
        return lane + swap, other - swap

    def forward_block(k):
        u = first_v[k] + mm(pick(recv_col[k], mesh_rows), rows_a[k])
        hidden, slope = silu_pair(u)
        slope_v[k] = slope.astype(BF16)
        unit, inv = normed(mm(hidden.astype(BF16), edge_out[...]))
        unit_v[k] = unit.astype(BF16)
        inv_v[k] = jnp.broadcast_to(inv, (cap, lanes))
        message = (edge_v[k].astype(F32) + vector(edge_gain) * unit).astype(BF16)
        sum_b.part[k] = mm(put(recv_row[pl.ds(k, 1), :], mesh_rows), message).astype(BF16)

    def backward_block(k):
        wanted = mm(pick(recv_col[k], mesh_rows), rows_c[k])
        wanted_v[k] = wanted.astype(BF16)
        dv = normed_back(wanted * vector(edge_gain), unit_v[k].astype(F32), inv_v[k][:, :1])
        dhidden = mm_t(dv.astype(BF16), edge_out[...])
        dfirst = (dhidden * slope_v[k].astype(F32)).astype(BF16)
        dfirst_v[k] = dfirst
        sum_d.part[k] = mm(put(recv_row[pl.ds(k, 1), :], mesh_rows), dfirst).astype(BF16)

    def all_blocks(block_fn, spread, sums):
        def step(t, _):
            first, second = step_blocks(t)

            @pl.when(t == 1)
            def _():
                for part in range(PARTS // 2, PARTS):
                    spread_near(part, spread)

            @pl.when(t == 3)
            def _():
                sum_near(0, sums)
                sum_near(1, sums)
                for part in range(PARTS // 2, PARTS):
                    spread_far(part, spread)
                spread_whole(first, spread)

            block_fn(first)

            @pl.when(t == 0)
            def _():
                for part in range(PARTS // 2):
                    spread_near(part, spread)

            @pl.when(t == 2)
            def _():
                for part in range(PARTS // 2):
                    spread_far(part, spread)

            @pl.when(t == 3)
            def _():
                pair_copy(first, sums).start()
                sum_cross(sums)

            @pl.when(jnp.logical_or(t < 3, core == 0))
            def _():
                spread_whole(second, spread)

            block_fn(second)

            @pl.when(t < 3)
            def _():
                pair_copy(second, sums).start()

            return 0

        lax.fori_loop(0, blocks // 2, step, 0)
        sum_far(sums)

    all_blocks(forward_block, spread_a, sum_b)

    def grid_step(i, _):
        rows = pl.ds(pl.multiple_of(i * cap, cap), cap)
        own = grid_v[rows, :]
        hidden, slope = silu_pair(mm(own, grid_in[...]) + vector(grid_bias))
        unit, inv = normed(mm(hidden.astype(BF16), grid_out[...]))
        grid_up[rows, :] = (own.astype(F32) + vector(grid_gain) * unit).astype(BF16)
        cot = grid_cot[rows, :].astype(F32)
        dv = normed_back(cot * vector(grid_gain), unit, inv)
        dfirst = (mm_t(dv.astype(BF16), grid_out[...]) * slope).astype(BF16)
        grid_grad[rows, :] = cot + mm_t(dfirst, grid_in[...])
        return 0

    grid_up_out = pltpu.make_async_copy(grid_up, grid_up_hbm, out_sem.at[blocks + 1])

    def grid_part():
        for load in loads[10:13]:
            load.wait()
        lax.fori_loop(0, grid_rows // cap, grid_step, 0)
        grid_up_out.start()

    for load in loads[7:10]:
        load.wait()
    node_first[...] = mm(mesh_v[...], node_in[wide, :]) + vector(node_bias)
    grid_part()
    sum_near_wait(sum_b)

    def node_step(part, _):
        own = part_rows(part)
        hidden, slope = silu_pair(node_first[own, :] + mm(summed(part, sum_b), node_in[mid, :]))
        unit, inv = normed(mm(hidden.astype(BF16), node_out[...]))
        cot = mesh_cot[own, :].astype(F32)
        dv = normed_back(cot * vector(node_gain), unit, inv)
        dfirst = (mm_t(dv.astype(BF16), node_out[...]) * slope).astype(BF16)
        rows_c[4, own] = mm_t(dfirst, node_in[mid, :]).astype(BF16)
        spread_own(part, spread_c)
        node_mesh_grad[own, :] = cot + mm_t(dfirst, node_in[wide, :])
        mesh_up[own, :] = (mesh_v[own, :].astype(F32) + vector(node_gain) * unit).astype(BF16)
        return 0

    lax.fori_loop(0, PARTS, node_step, 0)
    mesh_up_out = pltpu.make_async_copy(mesh_up, mesh_up_hbm, out_sem.at[blocks])
    mesh_up_out.start()

    all_blocks(backward_block, spread_c, sum_d)

    def edge_out_copy(k):
        return pltpu.make_async_copy(wanted_v.at[k], grad_edge_hbm.at[0, k], out_sem.at[k])

    def edge_step(k, _):
        wanted_v[k] = (
            wanted_v[k].astype(F32) + mm_t(dfirst_v[k], edge_in[wide, :])
        ).astype(BF16)
        edge_out_copy(k).start()
        return 0

    lax.fori_loop(0, blocks, edge_step, 0)

    def grid_sum_step(i, _):
        start = pl.multiple_of(i * cap, cap)
        rows = pl.ds(start, cap)
        value = mm(put(sender[0, 0:1, :], cap, start), dfirst_v[0])
        for k in range(1, blocks):
            value = value + mm(put(sender[0, k : k + 1, :], cap, start), dfirst_v[k])
        grad_grid[rows, :] = (
            grid_grad[rows, :] + mm_t(value.astype(BF16), edge_in[mid, :])
        ).astype(BF16)
        return 0

    lax.fori_loop(0, grid_rows // cap, grid_sum_step, 0)
    grad_grid_out = pltpu.make_async_copy(grad_grid, grad_grid_hbm, out_sem.at[blocks + 2])
    grad_grid_out.start()

    sum_near_wait(sum_d)
    for part in range(PARTS):
        own = part_rows(part)
        grad_mesh[own, :] = (
            node_mesh_grad[own, :] + mm_t(summed(part, sum_d), edge_in[last, :])
        ).astype(BF16)
    grad_mesh_out = pltpu.make_async_copy(grad_mesh, grad_mesh_hbm, out_sem.at[blocks + 3])
    grad_mesh_out.start()

    spread_sent(spread_a)
    sum_sent(sum_b)
    spread_sent(spread_c)
    sum_sent(sum_d)
    for k in range(blocks):
        edge_out_copy(k).wait()
    for copy in (mesh_up_out, grid_up_out, grad_grid_out, grad_mesh_out):
        copy.wait()


def place_kernel(*refs):
    sources, targets, held, load_sem, store_sem = refs[:5], refs[5:10], refs[10:15], refs[15], refs[16]
    views = [lambda ref, k=k: ref.at[0, k] for k in range(sources[4].shape[1])]
    work = [(4, view) for view in views] + [(i, lambda ref: ref) for i in (1, 2, 0, 3)]
    loads, stores = [], []
    for n, (i, view) in enumerate(work):
        loads.append(pltpu.make_async_copy(view(sources[i]), view(held[i]), load_sem.at[n]))
        stores.append(pltpu.make_async_copy(view(held[i]), view(targets[i]), store_sem.at[n]))
    for load in loads:
        load.start()
    for load, store in zip(loads, stores):
        load.wait()
        store.start()
    for store in stores:
        store.wait()


def on_device(
    grid_latent,
    mesh_latent,
    edge_latent,
    edge_sender,
    edge_receiver,
    edge_count,
    edge_in_weight,
    edge_bias,
    edge_out_weight,
    edge_gain,
    node_in_weight,
    node_bias,
    node_out_weight,
    node_gain,
    grid_in_weight,
    grid_bias,
    grid_out_weight,
    grid_gain,
    mesh_cotangent,
    grid_cotangent,
):
    _, blocks, cap, width = edge_latent.shape
    mesh_rows, grid_rows = mesh_latent.shape[0], grid_latent.shape[0]
    anywhere = pl.BlockSpec(memory_space=pl.ANY)
    vmem = pl.BlockSpec(memory_space=pltpu.VMEM)
    smem = pl.BlockSpec(memory_space=pltpu.SMEM)

    def buf(*shape, dtype=BF16):
        return pltpu.VMEM(shape, dtype)

    dma = pltpu.SemaphoreType.DMA
    slots = (blocks, cap, width)
    block = (mesh_rows, width)
    scratch = [
        buf(grid_rows, width),
        buf(mesh_rows, width),
        buf(*slots),
        buf(3 * width, width),
        buf(width, width),
        buf(2 * width, width),
        buf(width, width),
        buf(width, width),
        buf(width, width),
        buf(mesh_rows, width),
        buf(grid_rows, width),
        buf(grid_rows, width),
        buf(blocks, cap, dtype=jnp.int32),
        buf(blocks, cap, 128, dtype=jnp.int32),
        buf(blocks, cap, 128, dtype=jnp.int32),
        buf(*slots, dtype=F32),
        buf(*slots),
        buf(*slots),
        buf(blocks, cap, 128, dtype=F32),
        buf(*slots),
        buf(*slots),
        buf(blocks + 1, *block),
        buf(blocks + 1, *block),
        buf(*block, dtype=F32),
        buf(*block, dtype=F32),
        buf(grid_rows, width, dtype=F32),
        buf(*block),
        buf(grid_rows, width),
        buf(grid_rows, width),
        buf(*block),
        dma((13,)),
        dma((blocks + 4,)),
        dma((9, PARTS)),
        dma((blocks + 1, PARTS)),
        dma((9, PARTS)),
        dma((blocks + 1, PARTS)),
    ]
    sums = [
        buf(blocks, *block),
        buf(blocks // 2 + 1, *block),
        buf(3, *block),
        buf(*block),
        dma((blocks,)),
        dma((blocks // 2 + 1,)),
        dma((2,)),
        dma((PARTS,)),
        dma((PARTS,)),
        dma((PARTS,)),
        dma((PARTS,)),
    ]
    scratch = scratch + sums + sums
    outs = [
        jax.ShapeDtypeStruct(mesh_latent.shape, BF16),
        jax.ShapeDtypeStruct(grid_latent.shape, BF16),
        jax.ShapeDtypeStruct(grid_latent.shape, BF16),
        jax.ShapeDtypeStruct(mesh_latent.shape, BF16),
        jax.ShapeDtypeStruct(edge_latent.shape, BF16),
    ]
    results = pl.pallas_call(
        functools.partial(kernel, (blocks, cap, width, mesh_rows, grid_rows)),
        out_shape=outs,
        in_specs=[anywhere] * 3 + [vmem, vmem, smem] + [anywhere] * 6 + [vmem] * 6 + [anywhere] * 2,
        out_specs=[anywhere] * 5,
        scratch_shapes=scratch,
        compiler_params=pltpu.CompilerParams(
            collective_id=0, has_side_effects=True, vmem_limit_bytes=58 * 2**20
        ),
        cost_estimate=pl.CostEstimate(
            flops=13_000_000_000, bytes_accessed=16_000_000, transcendentals=3_000_000
        ),
        name="encoder",
    )(
        grid_latent,
        mesh_latent,
        edge_latent,
        edge_sender,
        edge_receiver,
        edge_count,
        edge_in_weight,
        edge_out_weight,
        node_in_weight,
        node_out_weight,
        grid_in_weight,
        grid_out_weight,
        edge_bias,
        edge_gain,
        node_bias,
        node_gain,
        grid_bias,
        grid_gain,
        mesh_cotangent,
        grid_cotangent,
    )
    return pl.pallas_call(
        place_kernel,
        out_shape=outs,
        in_specs=[anywhere] * 5,
        out_specs=[anywhere] * 5,
        scratch_shapes=[pltpu.VMEM(out.shape, out.dtype) for out in outs]
        + [dma((blocks + 4,)), dma((blocks + 4,))],
        compiler_params=pltpu.CompilerParams(vmem_limit_bytes=60 * 2**20),
        name="place",
    )(*results)


def solution(mesh):
    rows = P(("grid", "mesh"), None)
    wide = P(("grid", "mesh"), None, None)
    slots = P(("grid", "mesh"), None, None, None)
    return jax.shard_map(
        on_device,
        mesh=mesh,
        in_specs=(rows, rows, slots, wide, wide, rows) + (P(),) * 12 + (rows, rows),
        out_specs=(rows, rows, rows, rows, slots),
        check_vma=False,
    )
```

time: 101 us -> 87.1 us (0.86)
  the two profiles are of different devices: /device:TPU:1 before, /device:TPU:32 now
where the time goes in v1:
time: 87.1 us; the launch traced here: 86.9 us
  Pallas kernels  86.2 us (99%)
    pallas_call x1, Pallas kernels, on_device(): pl.pallas_call(functools.partial(kernel, (blocks, cap, width, mesh_rows,...  82.8 us
    pallas_call x1, Pallas kernels, on_device(): pl.pallas_call(place_kernel, out_shape=outs, in_specs=[anywhere] * 5, out...  3.38 us

profile of v1, /device:TPU:32, one launch (start us, length us, event | category | flops | bytes accessed | tf_op | source)
XLA Modules:
  0.0 86.9 jit_solution(2952520585667567331)
XLA Ops:
  0.6 82.8 %encoder.1 = (bf16[320,512]{1,0:T(8,128)(2,1)}, bf16[512,512]{1,0:T(8,128)(2,1)}, bf16[512,512]{1,0:T(8,128)(2,1)}, bf16[320,512]{1,0:T(8,128)(2,1)}, bf16[1,8,256,512]{3,2,1,0:T(8,128)(2,1)}) custom-call(bf16[512,512]{1,0:T(8,128)(2,1)} %grid_hbm.1, bf16[320,512]{1,0:T(8,128)(2,1)} %mesh_hbm.1, bf16[1,8,256,512]{3,2,1,0:T(8,128)(2,1)} %edge_hbm.1, ...), custom_call_target="tpu_custom_call" | custom-call | flops 12999999488 | bytes 16000000 | tf_op jit(solution)/shard_map/encoder/pallas_call | solution.py:669
  83.5 3.4 %place.1 = (bf16[320,512]{1,0:T(8,128)(2,1)}, bf16[512,512]{1,0:T(8,128)(2,1)}, bf16[512,512]{1,0:T(8,128)(2,1)}, bf16[320,512]{1,0:T(8,128)(2,1)}, bf16[1,8,256,512]{3,2,1,0:T(8,128)(2,1)}) custom-call(bf16[320,512]{1,0:T(8,128)(2,1)} %get-tuple-element.10.refs_0_, bf16[512,512]{1,0:T(8,128)(2,1)} %get-tuple-element.11.refs_1_, ...), custom_call_target="tpu_custom_call" | custom-call | tf_op jit(solution)/shard_map/place/pallas_call | solution.py:704

commit v2 on v1

--- a/solution.py
+++ b/solution.py
@@ -43,21 +43,21 @@
     grid_hbm,
     mesh_hbm,
     edge_hbm,
-    sender,
-    receiver,
-    count,
+    sender_hbm,
+    receiver_hbm,
+    count_hbm,
     edge_in_hbm,
     edge_out_hbm,
     node_in_hbm,
     node_out_hbm,
     grid_in_hbm,
     grid_out_hbm,
-    edge_bias,
-    edge_gain,
-    node_bias,
-    node_gain,
-    grid_bias,
-    grid_gain,
+    edge_bias_hbm,
+    edge_gain_hbm,
+    node_bias_hbm,
+    node_gain_hbm,
+    grid_bias_hbm,
+    grid_gain_hbm,
     mesh_cot_hbm,
     grid_cot_hbm,
     mesh_up_hbm,
@@ -65,8 +65,16 @@
     grad_grid_hbm,
     grad_mesh_hbm,
     grad_edge_hbm,
+    sender,
+    receiver,
+    count,
+    edge_bias,
+    edge_gain,
+    node_bias,
+    node_gain,
+    grid_bias,
+    grid_gain,
     grid_v,
-    mesh_v,
     edge_v,
     edge_in,
     edge_out,
@@ -78,6 +86,7 @@
     grid_cot,
     grid_proj,
     recv_row,
+    lent_row,
     send_col,
     recv_col,
     first_v,
@@ -91,6 +100,7 @@
     node_first,
     node_mesh_grad,
     grid_grad,
+    grid_sum,
     mesh_up,
     grid_up,
     grad_grid,
@@ -101,6 +111,8 @@
     a_recv,
     c_send,
     c_recv,
+    lend_send,
+    lend_recv,
     *sum_refs,
 ):
     blocks, cap, width, mesh_rows, grid_rows = sizes
@@ -130,12 +142,12 @@
     mid = pl.ds(width, width)
     last = pl.ds(2 * width, width)
     pairs = [
-        (mesh_hbm, mesh_v),
-        (edge_in_hbm.at[last], edge_in.at[last]),
         (grid_hbm, grid_v),
         (edge_in_hbm.at[mid], edge_in.at[mid]),
         (edge_in_hbm.at[wide], edge_in.at[wide]),
-        (edge_hbm.at[0], edge_v),
+        (edge_hbm.at[0], edge_v.at[pl.ds(0, blocks)]),
+        (edge_in_hbm.at[last], edge_in.at[last]),
+        (mesh_hbm, rows_a.at[4]),
         (edge_out_hbm, edge_out),
         (node_in_hbm, node_in),
         (node_out_hbm, node_out),
@@ -144,12 +156,24 @@
         (grid_out_hbm, grid_out),
         (grid_cot_hbm, grid_cot),
     ]
+    small = [
+        (count_hbm, count),
+        (sender_hbm, sender),
+        (receiver_hbm, receiver),
+        (edge_bias_hbm, edge_bias),
+        (edge_gain_hbm, edge_gain),
+        (node_bias_hbm, node_bias),
+        (node_gain_hbm, node_gain),
+        (grid_bias_hbm, grid_bias),
+        (grid_gain_hbm, grid_gain),
+    ]
+    few = [
+        pltpu.make_async_copy(src, dst, load_sem.at[len(pairs) + i])
+        for i, (src, dst) in enumerate(small)
+    ]
     loads = [pltpu.make_async_copy(src, dst, load_sem.at[i]) for i, (src, dst) in enumerate(pairs)]
-    for load in loads[:2]:
-        load.start()
-
     barrier = pltpu.get_barrier_semaphore()
-    partners = [at(2), at(-2), at(4), at(-4), at(8), at(-8), twin]
+    partners = [at(2), at(-2), at(8), at(-8), twin]
     for partner in partners:
         pl.semaphore_signal(
             barrier, inc=1, device_id=partner, device_id_type=pl.DeviceIdType.MESH
@@ -157,22 +181,27 @@
 
     def vector(ref):
         return ref[...].astype(F32).reshape(1, width)
+
+    def part_rows(part):
+        rows = mesh_rows // PARTS
+        return pl.ds(pl.multiple_of(part * rows, rows), rows)
+
+    far = 8 - 8 * core
+    onward = 2 - 4 * core
 
     def spread_copy(i, part, spread):
         src, dst, device = [
             (4, 2, at(2)),
             (4, 6, at(-2)),
             (4, 3 + 2 * core, twin),
-            (2, 0, at(2)),
+            (2 + 4 * (1 - core), far, at(-onward)),
             (2, 1 + 2 * core, twin),
             (6, 5 + 2 * core, twin),
-            (6, 8, at(-2)),
-            (8 - 8 * core, 7 - 6 * core, twin),
-            (8, 0, at(8)),
+            (far, 7 - 6 * core, twin),
         ][i]
         own = part_rows(part)
         return remote(
-            spread.rows.at[src, own],
+            spread.own.at[own] if i < 3 else spread.rows.at[src, own],
             spread.rows.at[dst, own],
             spread.send.at[i, part],
             spread.recv.at[dst, part],
@@ -194,159 +223,134 @@
     def spread_near(part, spread):
         spread_arrived(2, part, spread)
         spread_arrived(6, part, spread)
-
-        @pl.when(core == 0)
-        def _():
-            spread_copy(6, part, spread).start()
-
-        @pl.when(core == 1)
-        def _():
-            spread_copy(3, part, spread).start()
-
-        spread_copy(4, part, spread).start()
-        spread_copy(5, part, spread).start()
+        for i in (3, 4, 5):
+            spread_copy(i, part, spread).start()
 
     def spread_far(part, spread):
-        @pl.when(core == 0)
-        def _():
-            spread_arrived(8, part, spread)
-            spread_copy(8, part, spread).start()
-
-        @pl.when(core == 1)
-        def _():
-            spread_arrived(0, part, spread)
-
-        spread_copy(7, part, spread).start()
+        spread_arrived(far, part, spread)
+        spread_copy(6, part, spread).start()
 
     def spread_sent(spread):
         for part in range(PARTS):
-            for i in (0, 1, 2, 4, 5, 7):
+            for i in range(7):
                 spread_copy(i, part, spread).wait_send()
-
-            @pl.when(core == 0)
-            def _():
-                spread_copy(6, part, spread).wait_send()
-                spread_copy(8, part, spread).wait_send()
-
-            @pl.when(core == 1)
-            def _():
-                spread_copy(3, part, spread).wait_send()
 
     def pair_copy(k, sums):
         slot = lax.div(k - 1 + 2 * core, 2)
         return remote(
-            sums.part.at[k], sums.pair.at[slot], sums.send.at[k], sums.pair_recv.at[slot], twin
+            sums.part.at[k], sums.pair.at[slot], sums.pair_send.at[k], sums.pair_recv.at[slot], twin
         )
 
     def pair_arrived(slot, sums):
         own = sums.pair.at[slot]
-        remote(own, own, sums.send.at[1], sums.pair_recv.at[slot], twin).wait_recv()
-
-    def near_copy(i, sums):
-        k, device = [(6, at(2)), (2, at(-2))][i]
-        return remote(
-            sums.part.at[k], sums.land.at[i], sums.send.at[k], sums.near_recv.at[i], device
-        )
-
-    def cross_copy(part, sums):
+        remote(own, own, sums.pair_send.at[1], sums.pair_recv.at[slot], twin).wait_recv()
+
+    early = 2 + 4 * core
+    late = 6 - 4 * core
+
+    def early_copy(part, sums):
         own = part_rows(part)
         return remote(
-            sums.pair.at[4, own],
-            sums.cross.at[own],
-            sums.cross_send.at[part],
-            sums.cross_recv.at[part],
-            at(8),
+            sums.part.at[early, own],
+            sums.land.at[1 - core, own],
+            sums.send.at[0, part],
+            sums.land_recv.at[1 - core, part],
+            at(-onward),
+        )
+
+    def late_copy(part, sums):
+        own = part_rows(part)
+        return remote(
+            sums.part.at[late, own],
+            sums.land.at[core, own],
+            sums.send.at[1, part],
+            sums.land_recv.at[core, part],
+            at(onward),
         )
 
     def far_copy(part, sums):
         own = part_rows(part)
         return remote(
-            sums.part.at[0, own],
-            sums.land.at[2, own],
-            sums.far_send.at[part],
-            sums.far_recv.at[part],
-            at(-4),
+            sums.part.at[far, own],
+            sums.cross.at[own],
+            sums.send.at[2, part],
+            sums.cross_recv.at[part],
+            at(onward),
         )
 
-    def sum_near(i, sums):
-        k = (6, 2)[i]
-        pair_arrived(k // 2, sums)
-        sums.part[k] = (sums.part[k].astype(F32) + sums.pair[k // 2].astype(F32)).astype(BF16)
-        near_copy(i, sums).start()
-
-    def sum_cross(sums):
-        @pl.when(core == 0)
-        def _():
-            pair_arrived(4, sums)
-            for part in range(PARTS):
-                cross_copy(part, sums).start()
+    def join(k, own, sums, *more):
+        value = sums.part[k, own].astype(F32) + sums.pair[lax.div(k, 2), own].astype(F32)
+        for other in more:
+            value = value + other.astype(F32)
+        sums.part[k, own] = value.astype(BF16)
+
+    def sum_early(sums):
+        pair_arrived(lax.div(early, 2), sums)
+        for part in range(PARTS):
+            join(early, part_rows(part), sums)
+            early_copy(part, sums).start()
 
     def sum_far(sums):
-        def join_part(part, more):
+        pair_arrived(lax.div(far, 2), sums)
+        for part in range(PARTS):
+            join(far, part_rows(part), sums)
+            far_copy(part, sums).start()
+
+    def sum_late(sums):
+        pair_arrived(lax.div(late, 2), sums)
+        pair_arrived(2, sums)
+        for part in range(PARTS):
             own = part_rows(part)
-            sums.part[0, own] = (sums.part[0, own].astype(F32) + more.astype(F32)).astype(BF16)
-            far_copy(part, sums).start()
-
-        @pl.when(core == 0)
-        def _():
-            for part in range(PARTS):
-                cross_copy(part, sums).wait_recv()
-                join_part(part, sums.cross[part_rows(part)])
-
-        @pl.when(core == 1)
-        def _():
-            pair_arrived(0, sums)
-            for part in range(PARTS):
-                join_part(part, sums.pair[0, part_rows(part)])
-
-    def sum_near_wait(sums):
-        pair_arrived(2, sums)
-        for i in (0, 1):
-            near_copy(i, sums).wait_recv()
+            far_copy(part, sums).wait_recv()
+            join(late, own, sums, sums.cross[own])
+            late_copy(part, sums).start()
 
     def summed(part, sums):
-        far_copy(part, sums).wait_recv()
         own = part_rows(part)
+        early_copy(part, sums).wait_recv()
+        late_copy(part, sums).wait_recv()
         value = sums.part[4, own].astype(F32) + sums.pair[2, own].astype(F32)
-        for i in range(3):
-            value = value + sums.land[i, own].astype(F32)
-        return value.astype(BF16)
+        return (value + sums.land[0, own].astype(F32) + sums.land[1, own].astype(F32)).astype(BF16)
 
     def sum_sent(sums):
         for k in (1, 3, 5, 7):
             pair_copy(k, sums).wait_send()
-        for i in (0, 1):
-            near_copy(i, sums).wait_send()
         for part in range(PARTS):
-            far_copy(part, sums).wait_send()
-
-        @pl.when(core == 0)
-        def _():
-            for part in range(PARTS):
-                cross_copy(part, sums).wait_send()
-
-    def part_rows(part):
-        rows = mesh_rows // PARTS
-        return pl.ds(pl.multiple_of(part * rows, rows), rows)
-
-    spread_a = SimpleNamespace(rows=rows_a, send=a_send, recv=a_recv)
-    spread_c = SimpleNamespace(rows=rows_c, send=c_send, recv=c_recv)
+            for copy in (early_copy, late_copy, far_copy):
+                copy(part, sums).wait_send()
+
+    spread_a = SimpleNamespace(own=mesh_hbm, rows=rows_a, send=a_send, recv=a_recv)
+    spread_c = SimpleNamespace(own=rows_c.at[4], rows=rows_c, send=c_send, recv=c_recv)
     sum_b, sum_d = [
         SimpleNamespace(
             part=refs[0],
             pair=refs[1],
             land=refs[2],
             cross=refs[3],
-            send=refs[4],
+            pair_send=refs[4],
             pair_recv=refs[5],
-            near_recv=refs[6],
-            far_send=refs[7],
-            far_recv=refs[8],
-            cross_send=refs[9],
-            cross_recv=refs[10],
+            send=refs[6],
+            land_recv=refs[7],
+            cross_recv=refs[8],
         )
-        for refs in (sum_refs[:11], sum_refs[11:])
+        for refs in (sum_refs[:9], sum_refs[9:])
     ]
+
+    def lend_copy(i):
+        src, dst, shift = [
+            (edge_v.at[0], edge_v.at[blocks], -8),
+            (first_v.at[0], first_v.at[blocks], -8),
+            (recv_row.at[pl.ds(0, blocks)], lent_row, -8),
+            (wanted_v.at[blocks], wanted_v.at[0], 8),
+            (dfirst_v.at[blocks], dfirst_v.at[0], 8),
+        ][i]
+        return remote(src, dst, lend_send.at[i], lend_recv.at[i], at(shift))
+
+    def on_even(*steps):
+        @pl.when(core == 0)
+        def _():
+            for step in steps:
+                step()
 
     def pick(column, n):
         tiles = -(-n // lanes)
@@ -357,25 +361,29 @@
         ids = lax.broadcasted_iota(jnp.int32, (n, cap), 0) + start
         return jnp.where(ids == row, 1.0, 0.0).astype(BF16)
 
-    loads[0].wait()
-    loads[1].wait()
-    for load in loads[2:]:
+    for load in few:
         load.start()
-    rows_a[4] = mm(mesh_v[...], edge_in[last, :]).astype(BF16)
     pl.semaphore_wait(barrier, len(partners))
     for part in range(PARTS):
         spread_own(part, spread_a)
+    for load in loads:
+        load.start()
+
+    for load in few:
+        load.wait()
 
     slot_index = lax.broadcasted_iota(jnp.int32, (1, cap), 1)
     for k in range(blocks):
         recv_row[k : k + 1, :] = jnp.where(slot_index < count[0, k], receiver[0, k : k + 1, :], -1)
-    for src, dst in ((sender[0], send_col), (recv_row[...], recv_col)):
+    on_even(lend_copy(2).start)
+    for src, dst in ((sender[0], send_col), (recv_row[:blocks, :], recv_col)):
         turned = jnp.transpose(src)
         for k in range(blocks):
             dst[k] = jnp.broadcast_to(turned[:, k : k + 1], (cap, lanes))
 
-    for load in loads[2:6]:
+    for load in loads[:4]:
         load.wait()
+    on_even(lend_copy(0).start)
     grid_proj[...] = mm(grid_v[...], edge_in[mid, :]).astype(BF16)
 
     def first_step(k, _):
@@ -383,20 +391,31 @@
             mm(edge_v[k], edge_in[wide, :])
             + mm(pick(send_col[k], grid_rows), grid_proj[...])
             + vector(edge_bias)
-        )
+        ).astype(BF16)
+
+        @pl.when(jnp.logical_and(k == 0, core == 0))
+        def _():
+            lend_copy(1).start()
+
         return 0
 
-    lax.fori_loop(0, blocks, first_step, 0)
-    loads[6].wait()
-
-    def step_blocks(t):
+    lax.fori_loop(0, blocks // 2, first_step, 0)
+    for part in range(PARTS // 2):
+        spread_near(part, spread_a)
+    lax.fori_loop(blocks // 2, blocks, first_step, 0)
+    for load in loads[4:7]:
+        load.wait()
+
+    def step_blocks(t, swap):
         lane = lax.rem(4 + t + t * t, 8)
         other = lax.rem(lane + 9 - 2 * core, 8)
-        swap = lax.div(t, 3) * (other - lane)
-        return lane + swap, other - swap
+        lane = lane + lax.div(t, 3) * far
+        move = (lax.div(t, 3) * (1 - core) if swap else 0) * (other - lane)
+        return lane + move, other - move
 
     def forward_block(k):
-        u = first_v[k] + mm(pick(recv_col[k], mesh_rows), rows_a[k])
+        joined = mm(pick(recv_col[k], mesh_rows), rows_a[k]).astype(BF16)
+        u = first_v[k].astype(F32) + mm(joined, edge_in[last, :])
         hidden, slope = silu_pair(u)
         slope_v[k] = slope.astype(BF16)
         unit, inv = normed(mm(hidden.astype(BF16), edge_out[...]))
@@ -414,9 +433,9 @@
         dfirst_v[k] = dfirst
         sum_d.part[k] = mm(put(recv_row[pl.ds(k, 1), :], mesh_rows), dfirst).astype(BF16)
 
-    def all_blocks(block_fn, spread, sums):
+    def all_blocks(block_fn, spread, sums, after_own, before_lent, after_lent, swap):
         def step(t, _):
-            first, second = step_blocks(t)
+            first, second = step_blocks(t, swap)
 
             @pl.when(t == 1)
             def _():
@@ -425,18 +444,20 @@
 
             @pl.when(t == 3)
             def _():
-                sum_near(0, sums)
-                sum_near(1, sums)
+                sum_early(sums)
                 for part in range(PARTS // 2, PARTS):
                     spread_far(part, spread)
-                spread_whole(first, spread)
+                if swap:
+                    on_even(functools.partial(spread_whole, 1, spread))
+                else:
+                    on_even(*before_lent)
 
             block_fn(first)
 
             @pl.when(t == 0)
             def _():
-                for part in range(PARTS // 2):
-                    spread_near(part, spread)
+                for step in after_own:
+                    step()
 
             @pl.when(t == 2)
             def _():
@@ -445,16 +466,20 @@
 
             @pl.when(t == 3)
             def _():
-                pair_copy(first, sums).start()
-                sum_cross(sums)
-
-            @pl.when(jnp.logical_or(t < 3, core == 0))
+                if swap:
+                    on_even(pair_copy(1, sums).start, *before_lent)
+                else:
+                    on_even(*after_lent)
+
+            twin_second = jnp.logical_or(t < 3, core == 1) if swap else t >= 0
+
+            @pl.when(twin_second)
             def _():
                 spread_whole(second, spread)
 
             block_fn(second)
 
-            @pl.when(t < 3)
+            @pl.when(twin_second)
             def _():
                 pair_copy(second, sums).start()
 
@@ -463,7 +488,20 @@
         lax.fori_loop(0, blocks // 2, step, 0)
         sum_far(sums)
 
-    all_blocks(forward_block, spread_a, sum_b)
+    def lent_columns():
+        recv_row[blocks : blocks + 1, :] = lent_row[0:1, :]
+        turned = jnp.transpose(lent_row[...])
+        recv_col[blocks] = jnp.broadcast_to(turned[:, 0:1], (cap, lanes))
+
+    all_blocks(
+        forward_block,
+        spread_a,
+        sum_b,
+        [],
+        [lend_copy(i).wait_recv for i in (0, 1, 2)] + [lent_columns],
+        [],
+        True,
+    )
 
     def grid_step(i, _):
         rows = pl.ds(pl.multiple_of(i * cap, cap), cap)
@@ -487,9 +525,9 @@
 
     for load in loads[7:10]:
         load.wait()
-    node_first[...] = mm(mesh_v[...], node_in[wide, :]) + vector(node_bias)
+    node_first[...] = mm(rows_a[4], node_in[wide, :]) + vector(node_bias)
     grid_part()
-    sum_near_wait(sum_b)
+    sum_late(sum_b)
 
     def node_step(part, _):
         own = part_rows(part)
@@ -501,43 +539,60 @@
         rows_c[4, own] = mm_t(dfirst, node_in[mid, :]).astype(BF16)
         spread_own(part, spread_c)
         node_mesh_grad[own, :] = cot + mm_t(dfirst, node_in[wide, :])
-        mesh_up[own, :] = (mesh_v[own, :].astype(F32) + vector(node_gain) * unit).astype(BF16)
+        mesh_up[own, :] = (rows_a[4, own].astype(F32) + vector(node_gain) * unit).astype(BF16)
         return 0
 
     lax.fori_loop(0, PARTS, node_step, 0)
     mesh_up_out = pltpu.make_async_copy(mesh_up, mesh_up_hbm, out_sem.at[blocks])
     mesh_up_out.start()
 
-    all_blocks(backward_block, spread_c, sum_d)
+    all_blocks(
+        backward_block,
+        spread_c,
+        sum_d,
+        [functools.partial(spread_near, part, spread_c) for part in range(PARTS // 2)],
+        [],
+        [lend_copy(3).start, lend_copy(4).start],
+        False,
+    )
 
     def edge_out_copy(k):
         return pltpu.make_async_copy(wanted_v.at[k], grad_edge_hbm.at[0, k], out_sem.at[k])
 
-    def edge_step(k, _):
+    def edge_step(i, _):
+        k = lax.rem(i + 1, blocks)
         wanted_v[k] = (
             wanted_v[k].astype(F32) + mm_t(dfirst_v[k], edge_in[wide, :])
         ).astype(BF16)
         edge_out_copy(k).start()
         return 0
 
-    lax.fori_loop(0, blocks, edge_step, 0)
-
     def grid_sum_step(i, _):
         start = pl.multiple_of(i * cap, cap)
+        value = mm(put(sender[0, 1:2, :], cap, start), dfirst_v[1])
+        for k in range(2, blocks):
+            value = value + mm(put(sender[0, k : k + 1, :], cap, start), dfirst_v[k])
+        grid_sum[pl.ds(start, cap), :] = value
+        return 0
+
+    def grid_last_step(i, _):
+        start = pl.multiple_of(i * cap, cap)
         rows = pl.ds(start, cap)
-        value = mm(put(sender[0, 0:1, :], cap, start), dfirst_v[0])
-        for k in range(1, blocks):
-            value = value + mm(put(sender[0, k : k + 1, :], cap, start), dfirst_v[k])
+        value = grid_sum[rows, :] + mm(put(sender[0, 0:1, :], cap, start), dfirst_v[0])
         grad_grid[rows, :] = (
             grid_grad[rows, :] + mm_t(value.astype(BF16), edge_in[mid, :])
         ).astype(BF16)
         return 0
 
+    lax.fori_loop(0, blocks - 1, edge_step, 0)
+    sum_late(sum_d)
     lax.fori_loop(0, grid_rows // cap, grid_sum_step, 0)
+    on_even(lend_copy(3).wait_recv, lend_copy(4).wait_recv)
+    lax.fori_loop(blocks - 1, blocks, edge_step, 0)
+    lax.fori_loop(0, grid_rows // cap, grid_last_step, 0)
     grad_grid_out = pltpu.make_async_copy(grad_grid, grad_grid_hbm, out_sem.at[blocks + 2])
     grad_grid_out.start()
 
-    sum_near_wait(sum_d)
     for part in range(PARTS):
         own = part_rows(part)
         grad_mesh[own, :] = (
@@ -550,6 +605,7 @@
     sum_sent(sum_b)
     spread_sent(spread_c)
     sum_sent(sum_d)
+    on_even(*[lend_copy(i).wait_send for i in range(5)])
     for k in range(blocks):
         edge_out_copy(k).wait()
     for copy in (mesh_up_out, grid_up_out, grad_grid_out, grad_mesh_out):
@@ -598,19 +654,25 @@
     _, blocks, cap, width = edge_latent.shape
     mesh_rows, grid_rows = mesh_latent.shape[0], grid_latent.shape[0]
     anywhere = pl.BlockSpec(memory_space=pl.ANY)
-    vmem = pl.BlockSpec(memory_space=pltpu.VMEM)
-    smem = pl.BlockSpec(memory_space=pltpu.SMEM)
 
     def buf(*shape, dtype=BF16):
         return pltpu.VMEM(shape, dtype)
 
     dma = pltpu.SemaphoreType.DMA
-    slots = (blocks, cap, width)
+    more_slots = (blocks + 1, cap, width)
     block = (mesh_rows, width)
     scratch = [
+        buf(*edge_sender.shape, dtype=jnp.int32),
+        buf(*edge_receiver.shape, dtype=jnp.int32),
+        pltpu.SMEM(edge_count.shape, jnp.int32),
+        buf(width),
+        buf(width),
+        buf(width),
+        buf(width),
+        buf(width),
+        buf(width),
         buf(grid_rows, width),
-        buf(mesh_rows, width),
-        buf(*slots),
+        buf(*more_slots),
         buf(3 * width, width),
         buf(width, width),
         buf(2 * width, width),
@@ -620,42 +682,44 @@
         buf(mesh_rows, width),
         buf(grid_rows, width),
         buf(grid_rows, width),
+        buf(2 * blocks, cap, dtype=jnp.int32),
         buf(blocks, cap, dtype=jnp.int32),
         buf(blocks, cap, 128, dtype=jnp.int32),
-        buf(blocks, cap, 128, dtype=jnp.int32),
-        buf(*slots, dtype=F32),
-        buf(*slots),
-        buf(*slots),
-        buf(blocks, cap, 128, dtype=F32),
-        buf(*slots),
-        buf(*slots),
+        buf(blocks + 1, cap, 128, dtype=jnp.int32),
+        buf(*more_slots),
+        buf(*more_slots),
+        buf(*more_slots),
+        buf(blocks + 1, cap, 128, dtype=F32),
+        buf(*more_slots),
+        buf(*more_slots),
         buf(blocks + 1, *block),
         buf(blocks + 1, *block),
         buf(*block, dtype=F32),
         buf(*block, dtype=F32),
         buf(grid_rows, width, dtype=F32),
+        buf(grid_rows, width, dtype=F32),
         buf(*block),
         buf(grid_rows, width),
         buf(grid_rows, width),
         buf(*block),
-        dma((13,)),
+        dma((22,)),
         dma((blocks + 4,)),
-        dma((9, PARTS)),
+        dma((7, PARTS)),
         dma((blocks + 1, PARTS)),
-        dma((9, PARTS)),
+        dma((7, PARTS)),
         dma((blocks + 1, PARTS)),
+        dma((5,)),
+        dma((5,)),
     ]
     sums = [
-        buf(blocks, *block),
+        buf(blocks + 1, *block),
         buf(blocks // 2 + 1, *block),
-        buf(3, *block),
+        buf(2, *block),
         buf(*block),
         dma((blocks,)),
         dma((blocks // 2 + 1,)),
-        dma((2,)),
-        dma((PARTS,)),
-        dma((PARTS,)),
-        dma((PARTS,)),
+        dma((3, PARTS)),
+        dma((2, PARTS)),
         dma((PARTS,)),
     ]
     scratch = scratch + sums + sums
@@ -669,7 +733,7 @@
     results = pl.pallas_call(
         functools.partial(kernel, (blocks, cap, width, mesh_rows, grid_rows)),
         out_shape=outs,
-        in_specs=[anywhere] * 3 + [vmem, vmem, smem] + [anywhere] * 6 + [vmem] * 6 + [anywhere] * 2,
+        in_specs=[anywhere] * 20,
         out_specs=[anywhere] * 5,
         scratch_shapes=scratch,
         compiler_params=pltpu.CompilerParams(

time: 87.1 us -> 86.1 us (0.989)
  Pallas kernels: 86.2 us -> 85.2 us
    pallas_call x1, Pallas kernels: 82.8 us -> 81.8 us  [on_device(): pl.pallas_call(functools.partial(kernel, (blocks, cap, width, mesh_rows,...]
where the time goes in v2:
time: 86.1 us; the launch traced here: 85.8 us
  Pallas kernels  85.2 us (99%)
    pallas_call x1, Pallas kernels, on_device(): pl.pallas_call(functools.partial(kernel, (blocks, cap, width, mesh_rows,...  81.8 us
    pallas_call x1, Pallas kernels, on_device(): pl.pallas_call(place_kernel, out_shape=outs, in_specs=[anywhere] * 5, out...  3.38 us

profile of v2, /device:TPU:32, one launch (start us, length us, event | category | flops | bytes accessed | tf_op | source)
XLA Modules:
  0.0 85.8 jit_solution(1525914057264529317)
XLA Ops:
  0.6 81.8 %encoder.1 = (bf16[320,512]{1,0:T(8,128)(2,1)}, bf16[512,512]{1,0:T(8,128)(2,1)}, bf16[512,512]{1,0:T(8,128)(2,1)}, bf16[320,512]{1,0:T(8,128)(2,1)}, bf16[1,8,256,512]{3,2,1,0:T(8,128)(2,1)}) custom-call(bf16[512,512]{1,0:T(8,128)(2,1)} %grid_hbm.1, bf16[320,512]{1,0:T(8,128)(2,1)} %mesh_hbm.1, bf16[1,8,256,512]{3,2,1,0:T(8,128)(2,1)} %edge_hbm.1, ...), custom_call_target="tpu_custom_call" | custom-call | flops 12999999488 | bytes 16000000 | tf_op jit(solution)/shard_map/encoder/pallas_call | solution.py:733
  82.4 3.4 %place.1 = (bf16[320,512]{1,0:T(8,128)(2,1)}, bf16[512,512]{1,0:T(8,128)(2,1)}, bf16[512,512]{1,0:T(8,128)(2,1)}, bf16[320,512]{1,0:T(8,128)(2,1)}, bf16[1,8,256,512]{3,2,1,0:T(8,128)(2,1)}) custom-call(bf16[320,512]{1,0:T(8,128)(2,1)} %get-tuple-element.10.refs_0_, bf16[512,512]{1,0:T(8,128)(2,1)} %get-tuple-element.11.refs_1_, ...), custom_call_target="tpu_custom_call" | custom-call | tf_op jit(solution)/shard_map/place/pallas_call | solution.py:768

commit v3 on v2

--- a/solution.py
+++ b/solution.py
@@ -60,11 +60,11 @@
     grid_gain_hbm,
     mesh_cot_hbm,
     grid_cot_hbm,
-    mesh_up_hbm,
-    grid_up_hbm,
-    grad_grid_hbm,
-    grad_mesh_hbm,
-    grad_edge_hbm,
+    mesh_up,
+    grid_up,
+    grad_grid,
+    grad_mesh,
+    grad_edge,
     sender,
     receiver,
     count,
@@ -101,12 +101,7 @@
     node_mesh_grad,
     grid_grad,
     grid_sum,
-    mesh_up,
-    grid_up,
-    grad_grid,
-    grad_mesh,
     load_sem,
-    out_sem,
     a_send,
     a_recv,
     c_send,
@@ -346,6 +341,16 @@
         ][i]
         return remote(src, dst, lend_send.at[i], lend_recv.at[i], at(shift))
 
+    last_z = lax.div(lax.axis_index("mesh"), 2) == lax.div(fast, 2) - 1
+
+    def give_back(later):
+        if not later:
+            lend_copy(3).start()
+
+        @pl.when(last_z == later)
+        def _():
+            lend_copy(4).start()
+
     def on_even(*steps):
         @pl.when(core == 0)
         def _():
@@ -515,13 +520,11 @@
         grid_grad[rows, :] = cot + mm_t(dfirst, grid_in[...])
         return 0
 
-    grid_up_out = pltpu.make_async_copy(grid_up, grid_up_hbm, out_sem.at[blocks + 1])
 
     def grid_part():
         for load in loads[10:13]:
             load.wait()
         lax.fori_loop(0, grid_rows // cap, grid_step, 0)
-        grid_up_out.start()
 
     for load in loads[7:10]:
         load.wait()
@@ -543,8 +546,6 @@
         return 0
 
     lax.fori_loop(0, PARTS, node_step, 0)
-    mesh_up_out = pltpu.make_async_copy(mesh_up, mesh_up_hbm, out_sem.at[blocks])
-    mesh_up_out.start()
 
     all_blocks(
         backward_block,
@@ -552,19 +553,15 @@
         sum_d,
         [functools.partial(spread_near, part, spread_c) for part in range(PARTS // 2)],
         [],
-        [lend_copy(3).start, lend_copy(4).start],
+        [functools.partial(give_back, False)],
         False,
     )
 
-    def edge_out_copy(k):
-        return pltpu.make_async_copy(wanted_v.at[k], grad_edge_hbm.at[0, k], out_sem.at[k])
-
     def edge_step(i, _):
         k = lax.rem(i + 1, blocks)
-        wanted_v[k] = (
+        grad_edge[0, k] = (
             wanted_v[k].astype(F32) + mm_t(dfirst_v[k], edge_in[wide, :])
         ).astype(BF16)
-        edge_out_copy(k).start()
         return 0
 
     def grid_sum_step(i, _):
@@ -586,47 +583,32 @@
 
     lax.fori_loop(0, blocks - 1, edge_step, 0)
     sum_late(sum_d)
+    on_even(functools.partial(give_back, True))
     lax.fori_loop(0, grid_rows // cap, grid_sum_step, 0)
     on_even(lend_copy(3).wait_recv, lend_copy(4).wait_recv)
     lax.fori_loop(blocks - 1, blocks, edge_step, 0)
     lax.fori_loop(0, grid_rows // cap, grid_last_step, 0)
-    grad_grid_out = pltpu.make_async_copy(grad_grid, grad_grid_hbm, out_sem.at[blocks + 2])
-    grad_grid_out.start()
 
     for part in range(PARTS):
         own = part_rows(part)
         grad_mesh[own, :] = (
             node_mesh_grad[own, :] + mm_t(summed(part, sum_d), edge_in[last, :])
         ).astype(BF16)
-    grad_mesh_out = pltpu.make_async_copy(grad_mesh, grad_mesh_hbm, out_sem.at[blocks + 3])
-    grad_mesh_out.start()
 
     spread_sent(spread_a)
     sum_sent(sum_b)
     spread_sent(spread_c)
     sum_sent(sum_d)
     on_even(*[lend_copy(i).wait_send for i in range(5)])
-    for k in range(blocks):
-        edge_out_copy(k).wait()
-    for copy in (mesh_up_out, grid_up_out, grad_grid_out, grad_mesh_out):
+
+
+def place_kernel(*refs):
+    sources, targets, sems = refs[:5], refs[5:10], refs[10]
+    copies = [pltpu.make_async_copy(sources[i], targets[i], sems.at[i]) for i in range(5)]
+    for copy in copies:
+        copy.start()
+    for copy in copies:
         copy.wait()
-
-
-def place_kernel(*refs):
-    sources, targets, held, load_sem, store_sem = refs[:5], refs[5:10], refs[10:15], refs[15], refs[16]
-    views = [lambda ref, k=k: ref.at[0, k] for k in range(sources[4].shape[1])]
-    work = [(4, view) for view in views] + [(i, lambda ref: ref) for i in (1, 2, 0, 3)]
-    loads, stores = [], []
-    for n, (i, view) in enumerate(work):
-        loads.append(pltpu.make_async_copy(view(sources[i]), view(held[i]), load_sem.at[n]))
-        stores.append(pltpu.make_async_copy(view(held[i]), view(targets[i]), store_sem.at[n]))
-    for load in loads:
-        load.start()
-    for load, store in zip(loads, stores):
-        load.wait()
-        store.start()
-    for store in stores:
-        store.wait()
 
 
 def on_device(
@@ -698,12 +680,7 @@
         buf(*block, dtype=F32),
         buf(grid_rows, width, dtype=F32),
         buf(grid_rows, width, dtype=F32),
-        buf(*block),
-        buf(grid_rows, width),
-        buf(grid_rows, width),
-        buf(*block),
         dma((22,)),
-        dma((blocks + 4,)),
         dma((7, PARTS)),
         dma((blocks + 1, PARTS)),
         dma((7, PARTS)),
@@ -732,12 +709,12 @@
     ]
     results = pl.pallas_call(
         functools.partial(kernel, (blocks, cap, width, mesh_rows, grid_rows)),
-        out_shape=outs,
+        out_shape=[pltpu.VMEM(out.shape, out.dtype) for out in outs],
         in_specs=[anywhere] * 20,
-        out_specs=[anywhere] * 5,
+        out_specs=[pl.BlockSpec(memory_space=pltpu.VMEM)] * 5,
         scratch_shapes=scratch,
         compiler_params=pltpu.CompilerParams(
-            collective_id=0, has_side_effects=True, vmem_limit_bytes=58 * 2**20
+            collective_id=0, has_side_effects=True, vmem_limit_bytes=52 * 2**20
         ),
         cost_estimate=pl.CostEstimate(
             flops=13_000_000_000, bytes_accessed=16_000_000, transcendentals=3_000_000
@@ -770,9 +747,8 @@
         out_shape=outs,
         in_specs=[anywhere] * 5,
         out_specs=[anywhere] * 5,
-        scratch_shapes=[pltpu.VMEM(out.shape, out.dtype) for out in outs]
-        + [dma((blocks + 4,)), dma((blocks + 4,))],
-        compiler_params=pltpu.CompilerParams(vmem_limit_bytes=60 * 2**20),
+        scratch_shapes=[dma((5,))],
+        compiler_params=pltpu.CompilerParams(vmem_limit_bytes=16 * 2**20),
         name="place",
     )(*results)
 

time: 86.1 us -> 81.9 us (0.951)
  Pallas kernels: 85.2 us -> 80.2 us
    pallas_call x1, Pallas kernels: 81.8 us -> 78.2 us  [on_device(): pl.pallas_call(functools.partial(kernel, (blocks, cap, width, mesh_rows,...]
    pallas_call x1, Pallas kernels: 3.38 us -> 1.93 us  [on_device(): pl.pallas_call(place_kernel, out_shape=outs, in_specs=[anywhere] * 5, out...]
where the time goes in v3:
time: 81.9 us; the launch traced here: 80.8 us
  Pallas kernels  80.2 us (98%)
    pallas_call x1, Pallas kernels, on_device(): pl.pallas_call(functools.partial(kernel, (blocks, cap, width, mesh_rows,...  78.2 us
    pallas_call x1, Pallas kernels, on_device(): pl.pallas_call(place_kernel, out_shape=outs, in_specs=[anywhere] * 5, out...  1.93 us

profile of v3, /device:TPU:32, one launch (start us, length us, event | category | flops | bytes accessed | tf_op | source)
XLA Modules:
  0.0 80.8 jit_solution(14939688166887313131)
XLA Ops:
  0.6 78.2 %encoder.1 = (bf16[320,512]{1,0:T(8,128)(2,1)S(1)}, bf16[512,512]{1,0:T(8,128)(2,1)S(1)}, bf16[512,512]{1,0:T(8,128)(2,1)S(1)}, bf16[320,512]{1,0:T(8,128)(2,1)S(1)}, bf16[1,8,256,512]{3,2,1,0:T(8,128)(2,1)S(1)}) custom-call(bf16[512,512]{1,0:T(8,128)(2,1)} %grid_hbm.1, bf16[320,512]{1,0:T(8,128)(2,1)} %mesh_hbm.1, bf16[1,8,256,512]{3,2,1,0:T(8,128)(2,1)} %edge_hbm.1, ...), custom_call_target="tpu_custom_call" | custom-call | flops 12999999488 | bytes 16000000 | tf_op jit(solution)/shard_map/encoder/pallas_call | solution.py:710
  78.9 1.9 %place.1 = (bf16[320,512]{1,0:T(8,128)(2,1)}, bf16[512,512]{1,0:T(8,128)(2,1)}, bf16[512,512]{1,0:T(8,128)(2,1)}, bf16[320,512]{1,0:T(8,128)(2,1)}, bf16[1,8,256,512]{3,2,1,0:T(8,128)(2,1)}) custom-call(bf16[320,512]{1,0:T(8,128)(2,1)S(1)} %get-tuple-element.10.refs_0_, bf16[512,512]{1,0:T(8,128)(2,1)S(1)} %get-tuple-element.11.refs_1_, ...), custom_call_target="tpu_custom_call" | custom-call | tf_op jit(solution)/shard_map/place/pallas_call | solution.py:745

commit v4 on v3

--- a/solution.py
+++ b/solution.py
@@ -412,9 +412,9 @@
         load.wait()
 
     def step_blocks(t, swap):
-        lane = lax.rem(4 + t + t * t, 8)
-        other = lax.rem(lane + 9 - 2 * core, 8)
-        lane = lane + lax.div(t, 3) * far
+        turn = lax.rem(4 + t + t * t, 8)
+        lane = turn + (1 - core) * (8 - 2 * turn)
+        other = (1 - core) * (turn + 1) + core * (7 - turn)
         move = (lax.div(t, 3) * (1 - core) if swap else 0) * (other - lane)
         return lane + move, other - move
 
@@ -449,7 +449,6 @@
 
             @pl.when(t == 3)
             def _():
-                sum_early(sums)
                 for part in range(PARTS // 2, PARTS):
                     spread_far(part, spread)
                 if swap:
@@ -466,6 +465,7 @@
 
             @pl.when(t == 2)
             def _():
+                sum_early(sums)
                 for part in range(PARTS // 2):
                     spread_far(part, spread)
 

time: 81.9 us -> 80.9 us (0.988)
  Pallas kernels: 80.2 us -> 79.2 us
    pallas_call x1, Pallas kernels: 78.2 us -> 77.3 us  [on_device(): pl.pallas_call(functools.partial(kernel, (blocks, cap, width, mesh_rows,...]
where the time goes in v4:
time: 80.9 us; the launch traced here: 79.9 us
  Pallas kernels  79.2 us (98%)
    pallas_call x1, Pallas kernels, on_device(): pl.pallas_call(functools.partial(kernel, (blocks, cap, width, mesh_rows,...  77.3 us
    pallas_call x1, Pallas kernels, on_device(): pl.pallas_call(place_kernel, out_shape=outs, in_specs=[anywhere] * 5, out...  1.93 us

profile of v4, /device:TPU:32, one launch (start us, length us, event | category | flops | bytes accessed | tf_op | source)
XLA Modules:
  0.0 79.9 jit_solution(283831961913053298)
XLA Ops:
  0.6 77.3 %encoder.1 = (bf16[320,512]{1,0:T(8,128)(2,1)S(1)}, bf16[512,512]{1,0:T(8,128)(2,1)S(1)}, bf16[512,512]{1,0:T(8,128)(2,1)S(1)}, bf16[320,512]{1,0:T(8,128)(2,1)S(1)}, bf16[1,8,256,512]{3,2,1,0:T(8,128)(2,1)S(1)}) custom-call(bf16[512,512]{1,0:T(8,128)(2,1)} %grid_hbm.1, bf16[320,512]{1,0:T(8,128)(2,1)} %mesh_hbm.1, bf16[1,8,256,512]{3,2,1,0:T(8,128)(2,1)} %edge_hbm.1, ...), custom_call_target="tpu_custom_call" | custom-call | flops 12999999488 | bytes 16000000 | tf_op jit(solution)/shard_map/encoder/pallas_call | solution.py:710
  77.9 1.9 %place.1 = (bf16[320,512]{1,0:T(8,128)(2,1)}, bf16[512,512]{1,0:T(8,128)(2,1)}, bf16[512,512]{1,0:T(8,128)(2,1)}, bf16[320,512]{1,0:T(8,128)(2,1)}, bf16[1,8,256,512]{3,2,1,0:T(8,128)(2,1)}) custom-call(bf16[320,512]{1,0:T(8,128)(2,1)S(1)} %get-tuple-element.10.refs_0_, bf16[512,512]{1,0:T(8,128)(2,1)S(1)} %get-tuple-element.11.refs_1_, ...), custom_call_target="tpu_custom_call" | custom-call | tf_op jit(solution)/shard_map/place/pallas_call | solution.py:745
